TPU v7x, 256 devices: a whole 4x4x8 slice. The times are simulated.
256 devices in a mesh: row: 8 (over x_lo, y), col: 32 (over z, x_hi, core).
Axes of the slice: x: 4 (x_hi: 2, x_lo: 2; x = x_hi * 2 + x_lo), y: 4, z: 8, core: 2. Of those that a mesh axis runs over, the one named last changes fastest.
Arguments:
- a_values: bfloat16 [32, 128, 4096], P('col', 'row'), may hold values from -0.09375 to 0.09375
- a_rows: int32 [32, 128], P('col', 'row'), may hold values from 0 to 3, as said below
- a_cols: int32 [32, 128], P('col', 'row'), may hold values from 0 to 15, as said below
- a_count: int32 [32, 8], P('col', 'row'), may hold values from 4 to 16, as said below
- p_values: bfloat16 [8, 128, 4096], P('row', 'col'), may hold values from -1.5 to 1.5
- p_rows: int32 [8, 128], P('row', 'col'), may hold values from 0 to 15, as said below
- p_cols: int32 [8, 128], P('row', 'col'), may hold values from 0 to 1, as said below
- p_count: int32 [8, 32], P('row', 'col'), may hold values from 2 to 4, as said below
Outputs:
- coarse: float32 [4096, 4096], P('col', 'row')
Inputs may be any that keep to these rules, and one draw needn't show every extreme that they name: `a_rows`: block rows within a panel of 4. `a_cols`: block columns within a panel of 16; no (row, column) pair appears twice in one device's list, unused slots included. `a_count`: slots at or past the count are ignored; some device is full. `p_rows`: block rows within a panel of 16. `p_cols`: block columns within a panel of 2; no (row, column) pair appears twice in one device's list, unused slots included. `p_count`: slots at or past the count are ignored; some device is full.
All inputs are finite; a program needn't handle non-finite values.
Results may differ from a plain program's by a relative error of at most 0.01.
Values may be sent and summed in bfloat16 or wider, within the bound.
A program may use at most 128 MiB of HBM per device.

v0:
```python
import jax
import jax.numpy as jnp
from jax import lax
from jax.sharding import PartitionSpec as P

BS = 64
FB_DEV = 4
CB_DEV = 2


def broadcast(value, axis, source):
    kept = jnp.where(lax.axis_index(axis) == source, value, 0).astype(value.dtype)
    return lax.psum(kept, axis)


def block_grid(values, list_rows, list_cols, alive, height, breadth):
    slot_total = values.shape[0]
    blocks = (values * alive.astype(values.dtype)[:, None]).reshape(slot_total, BS, BS)
    layout = jnp.zeros((height, breadth, BS, BS), values.dtype).at[list_rows, list_cols].add(blocks)
    return layout.transpose(0, 2, 1, 3).reshape(height * BS, breadth * BS)


def shards(a_values, a_rows, a_cols, a_count, p_values, p_rows, p_cols, p_count):
    row_count = lax.axis_size("row")
    col_count = lax.axis_size("col")
    spread_ratio = col_count // row_count
    panel_rows = FB_DEV * spread_ratio
    slots_a = a_values.shape[1]
    slots_p = p_values.shape[1]
    alive_p = jnp.arange(slots_p) < p_count[0, 0]
    p_tile = block_grid(p_values[0], p_rows[0], p_cols[0], alive_p, panel_rows, CB_DEV)
    prolong = lax.all_gather(p_tile, "col", axis=1, tiled=True)
    alive_a = jnp.arange(slots_a) < a_count[0, 0]
    a_tile = block_grid(a_values[0], a_rows[0], a_cols[0], alive_a, FB_DEV, panel_rows)
    slab = prolong
    product_t = lax.psum_scatter(
        lax.dot_general(slab, a_tile, (((0,), (1,)), ((), ())), preferred_element_type=jnp.float32),
        "row",
        scatter_dimension=0,
        tiled=True,
    ).astype(jnp.bfloat16)
    col_index = lax.axis_index("col")
    own_rows = lax.dynamic_slice_in_dim(
        prolong, col_index % spread_ratio * (FB_DEV * BS), FB_DEV * BS, 0
    )
    restrict = broadcast(own_rows, "row", col_index // spread_ratio)
    slab = restrict
    return lax.psum_scatter(
        lax.dot_general(
            slab, product_t, (((0,), (1,)), ((), ())), preferred_element_type=jnp.float32
        ),
        "col",
        scatter_dimension=0,
        tiled=True,
    )


def solution(mesh):
    return jax.shard_map(
        shards,
        mesh=mesh,
        in_specs=(
            P("col", "row", None),
            P("col", "row"),
            P("col", "row"),
            P("col", "row"),
            P("row", "col", None),
            P("row", "col"),
            P("row", "col"),
            P("row", "col"),
        ),
        out_specs=P("col", "row"),
        check_vma=False,
    )
```

profile of v0, /device:TPU:4, one launch (start us, length us, event | category | flops | bytes accessed | tf_op | source)
XLA Modules:
  0.0 425.3 jit_solution(638443215750396073)
XLA Ops:
  6.5 0.0 all-gather.2.cloned.1.call-start
  7.2 0.9 squeeze.26
  8.1 0.7 fusion.4
  8.8 0.1 broadcast_multiply_fusion.1
  8.8 0.1 broadcast_in_dim.7
  9.0 0.8 scatter_fusion
  9.7 0.0 copy-start
  9.7 0.0 copy-start.1
  9.7 0.0 copy-start.2
  9.8 0.4 copy.10
  10.2 1.1 reshape.142
  11.3 0.0 all-gather.2.cloned.1.call-update
  11.3 0.0 all-reduce.2.cloned.1.call-start
  11.4 102.0 %all-gather.2.cloned.1.call-done = bf16[1024,4096]{0,1:T(8,128)(2,1)} async-done(((bf16[1024,128]{0,1:T(8,128)(2,1)}), bf16[1024,4096]{0,1:T(8,128)(2,1)}) %all-gather.2.cloned.1.call-update) | async-done | bytes 8388624 | tf_op jit(solution)/shard_map/all_gather | solution.py:32
  113.4 3.3 dynamic-slice_select_fusion
  116.7 0.0 all-reduce.2.cloned.1.call-update
  116.7 0.0 reduce-scatter.3.cloned.1.call-start
  117.4 0.0 copy-done
  117.4 0.2 squeeze.30
  117.7 0.0 copy-done.1
  117.7 0.0 copy-done.2
  117.7 0.1 broadcast_multiply_fusion
  117.8 0.2 broadcast_in_dim.18
  118.1 1.6 scatter_fusion.1
  119.6 0.7 copy.11
  120.3 0.7 reshape.143
  121.1 7.7 %fusion.6 = f32[4096,256]{1,0:T(8,128)} fusion(bf16[1024,4096]{0,1:T(8,128)(2,1)} %all-gather.2.cloned.1.call-done, bf16[256,1024]{1,0:T(8,128)(2,1)S(1)} %reshape.143), kind=kOutput, calls=%fused_computation.23 | convolution fusion | flops 2147483648 | bytes 13107200 | tf_op jit(solution)/shard_map/dot_general | solution.py:37
  128.8 0.0 reduce-scatter.3.cloned.1.call-update
  128.8 0.0 reduce-scatter.5.cloned.1.call-start
  128.8 73.8 %all-reduce.2.cloned.1.call-done = bf16[256,4096]{0,1:T(8,128)(2,1)} async-done(((bf16[256,4096]{0,1:T(8,128)(2,1)}), bf16[256,4096]{0,1:T(8,128)(2,1)}) %all-reduce.2.cloned.1.call-update) | async-done | bytes 2097168 | tf_op jit(solution)/shard_map/psum | solution.py:13
  202.6 58.5 %reduce-scatter.3.cloned.1.call-done = f32[512,256]{1,0:T(8,128)} async-done(((f32[4096,256]{1,0:T(8,128)}), f32[512,256]{1,0:T(8,128)}) %reduce-scatter.3.cloned.1.call-update) | async-done | bytes 524304 | tf_op jit(solution)/shard_map/reduce_scatter | solution.py:36
  261.1 6.2 %fusion = f32[4096,512]{1,0:T(8,128)} fusion(bf16[256,4096]{0,1:T(8,128)(2,1)} %all-reduce.2.cloned.1.call-done, f32[512,256]{1,0:T(8,128)} %reduce-scatter.3.cloned.1.call-done), kind=kOutput, calls=%fused_computation.3 | convolution fusion | flops 1073872896 | bytes 11010048 | tf_op jit(solution)/shard_map/dot_general | solution.py:49
  267.3 0.0 reduce-scatter.5.cloned.1.call-update
  267.4 151.4 %reduce-scatter.5.cloned.1.call-done = f32[128,512]{1,0:T(8,128)} async-done(((f32[4096,512]{1,0:T(8,128)}), f32[128,512]{1,0:T(8,128)}) %reduce-scatter.5.cloned.1.call-update) | async-done | bytes 262160 | tf_op jit(solution)/shard_map/reduce_scatter | solution.py:48
  (3 shorter events, 0.0 us)
Async XLA Ops:
  6.5 106.8 %all-gather.2.cloned.1.call-start = ((), (), s32[]{:S(2)}) async-start(), calls=%async_computation.2 | async-start | bytes 8650752 | tf_op jit(solution)/shard_map/all_gather | solution.py:32
  9.7 107.7 %copy-start = (bf16[1,16,4096]{2,1,0:T(8,128)(2,1)S(1)}, bf16[1,16,4096]{2,1,0:T(8,128)(2,1)}, u32[]{:S(2)}) copy-start(bf16[1,16,4096]{2,1,0:T(8,128)(2,1)} %param.8) | copy-start | bytes 393220
  9.7 107.9 %copy-start.1 = (s32[1,16]{1,0:T(1,128)S(1)}, s32[1,16]{1,0:T(1,128)}, u32[]{:S(2)}) copy-start(s32[1,16]{1,0:T(1,128)} %param.10) | copy-start | bytes 196
  9.7 107.9 %copy-start.2 = (s32[1,16]{1,0:T(1,128)S(1)}, s32[1,16]{1,0:T(1,128)}, u32[]{:S(2)}) copy-start(s32[1,16]{1,0:T(1,128)} %param.9) | copy-start | bytes 196
  11.3 191.3 %all-reduce.2.cloned.1.call-start = ((), (), s32[]{:S(2)}) async-start(), calls=%async_computation.3 | async-start | bytes 4194304 | tf_op jit(solution)/shard_map/psum | solution.py:13
  116.7 144.4 %reduce-scatter.3.cloned.1.call-start = ((), (), s32[]{:S(2)}) async-start(), calls=%async_computation.4 | async-start | bytes 4718592 | tf_op jit(solution)/shard_map/reduce_scatter | solution.py:36
  128.8 289.9 %reduce-scatter.5.cloned.1.call-start = ((), (), s32[]{:S(2)}) async-start(), calls=%async_computation.5 | async-start | bytes 8650752 | tf_op jit(solution)/shard_map/reduce_scatter | solution.py:48
Sparse Core Ops, SparseCore 0:
  11.4 101.9 all-gather.1
  116.8 85.7 all-reduce.1
  205.2 55.9 reduce-scatter.2
  267.5 151.2 reduce-scatter.4
where the time goes:
time: 427 us; the launch traced here: 425 us
  waiting for transfers between devices  386 us (90%)
  between operations  14.6 us (3%)
  matrix products  13.9 us (3%)
  other arithmetic  6.52 us (2%)
  local copies, waits for them, and re-layouts  4.37 us (1%)
    reduce_scatter x1, waiting for transfers between devices, shards(): lax.psum_scatter(lax.dot_general(slab, product_t, (((0,), (1,)), ((), ())...  151 us
    all_gather x1, waiting for transfers between devices, shards(): prolong = lax.all_gather(p_tile, 'col', axis=1, tiled=True)  102 us
    psum x1, waiting for transfers between devices, broadcast(): return lax.psum(kept, axis)  73.8 us
    reduce_scatter x1, waiting for transfers between devices, shards(): lax.psum_scatter(lax.dot_general(slab, a_tile, (((0,), (1,)), ((), ())),...  58.5 us
  transfers between devices with their start and end apart: 4, of which 4 were waited for; matrix products, arithmetic and copies ran while one was open for 3% of the time, Pallas kernels for 0%

commit v1 on v0

v1 whole, which is shorter than its diff:
```python
import functools

import jax
import jax.numpy as jnp
from jax import lax
from jax.experimental import pallas as pl
from jax.experimental.pallas import tpu as pltpu
from jax.sharding import PartitionSpec as P

BS = 64
FB_DEV = 4
CB_DEV = 2
Q = 4
SLOTS_A = 16
SLOTS_P = 4
PAIRS_A = SLOTS_A // 2
PAIRS_P = SLOTS_P // 2
LANES = 2 * BS
KEYS = 16
A_ROWS = PAIRS_A * BS + KEYS + SLOTS_A
P_ROWS = PAIRS_P * BS + KEYS
FINE = FB_DEV * BS
HALF = 2 * CB_DEV * BS
MESH = pl.DeviceIdType.MESH
BF16 = jnp.bfloat16
F32 = jnp.float32


def remote(src, dst, send, recv, target):
    return pltpu.make_async_remote_copy(
        src_ref=src, dst_ref=dst, send_sem=send, recv_sem=recv, device_id=target, device_id_type=MESH
    )


def swap_halves(x):
    return jnp.concatenate([x[:, BS:], x[:, :BS]], axis=1)


def tile_rows(row):
    return jnp.broadcast_to(row, (16, LANES)).astype(BF16)


def scaled(x, mask):
    return (x.reshape(BS // 16, 16, LANES) * mask[None]).reshape(BS, LANES)


def kernel(
    nr,
    ar, ac, an, pr, pc, pn, a_ref, p_ref, out_ref,
    abuf, zbuf, cbuf, tbuf, gbuf, left, rhs, restrict, acc, prod, outgoing, incoming, own,
    zs, zr, cs, cr, asnd, arcv, afs, afr, b2s, b2r, c2s, c2r, b3s, b3r, pgs, pgr, fs, fr,
):
    ny = nr // 2
    i = lax.axis_index("row")
    j = lax.axis_index("col")
    z, q = j // Q, j % Q
    xl, y = i // ny, i % ny
    mate = (1 - xl) * ny + y
    twin = q + 1 - 2 * (q % 2)
    far = (q + 2) % Q
    far_twin = (twin + 2) % Q
    at = lambda row, zz, qq: (row, zz * Q + qq)
    hop = lambda k, d: (k + d) % nr

    barrier = pltpu.get_barrier_semaphore()
    for d in range(1, nr):
        pl.semaphore_signal(barrier, inc=1, device_id=at(hop(i, d), z, q), device_id_type=MESH)
        pl.semaphore_signal(barrier, inc=1, device_id=at(i, hop(z, d), q), device_id_type=MESH)
    pl.semaphore_signal(barrier, inc=1, device_id=at(i, z, twin), device_id_type=MESH)
    pl.semaphore_signal(barrier, inc=1, device_id=at(i, z, far), device_id_type=MESH)

    lane = lax.broadcasted_iota(jnp.int32, (1, LANES), 1)
    second = lane >= BS
    half = second.astype(jnp.int32)
    rows_u = lax.broadcasted_iota(jnp.int32, (KEYS, LANES), 0)
    rows_s = lax.broadcasted_iota(jnp.int32, (SLOTS_A, LANES), 0)
    half_s = (lax.broadcasted_iota(jnp.int32, (SLOTS_A, LANES), 1) >= BS).astype(jnp.int32)
    p_keys = jnp.full((KEYS, LANES), -1, jnp.int32)
    for u in range(PAIRS_P):
        keys = [
            jnp.where(s < pn[0, 0], pr[0, s] * CB_DEV + pc[0, s], -1) for s in (2 * u, 2 * u + 1)
        ]
        p_keys = jnp.where(rows_u == u, jnp.where(second, keys[1], keys[0]), p_keys)
    tile = jnp.concatenate([p_ref[...], p_keys.astype(F32).astype(BF16)], axis=0)
    zbuf[z] = tile
    cbuf[i] = tile
    a_keys = jnp.full((KEYS, LANES), -1, jnp.int32)
    for u in range(PAIRS_A):
        keys = [jnp.where(s < an[0, 0], ar[0, s], -1) for s in (2 * u, 2 * u + 1)]
        a_keys = jnp.where(rows_u == u, jnp.where(second, keys[1], keys[0]), a_keys)
    a_cols = jnp.zeros((SLOTS_A, LANES), jnp.int32)
    for s in range(SLOTS_A):
        a_cols = jnp.where(rows_s == s, ac[0, s], a_cols)
    a_cols = a_cols * 2 + half_s
    abuf[i] = jnp.concatenate(
        [a_ref[...], a_keys.astype(F32).astype(BF16), a_cols.astype(F32).astype(BF16)], axis=0
    )

    pl.semaphore_wait(barrier, 2 * (nr - 1) + 2)

    sent = []

    def send(*args):
        copy = remote(*args)
        copy.start()
        sent.append(copy)

    for d in range(1, nr):
        to = hop(z, d)
        send(zbuf.at[z], zbuf.at[z], zs.at[to], zr.at[z], at(i, to, q))
    for d in range(1, nr):
        to = hop(i, d)
        send(cbuf.at[i], cbuf.at[i], cs.at[to], cr.at[i], at(to, z, q))
    send(abuf.at[i], abuf.at[i], asnd.at[0], arcv.at[0], at(mate, z, q))
    for e in range(1, ny):
        send(abuf.at[i], abuf.at[i], asnd.at[e], arcv.at[e], at(xl * ny + (y + e) % ny, z, q))

    for d in range(nr):
        k = hop(z, nr - d)
        if d:
            remote(zbuf.at[k], zbuf.at[k], zs.at[k], zr.at[k], at(i, k, q)).wait_recv()

        @pl.when(k == i)
        def _():
            gbuf[q, i] = zbuf[i]

        @pl.when(k != i)
        def _():
            remote(zbuf.at[k], gbuf.at[q, i], b2s.at[k], b2r.at[i], at(k, z, q)).start()

    remote(abuf.at[mate], abuf.at[mate], asnd.at[0], arcv.at[0], at(mate, z, q)).wait_recv()
    for e in range(1, ny):
        send(abuf.at[mate], abuf.at[mate], afs.at[e], afr.at[e], at(xl * ny + (y + e) % ny, z, q))

    for d in range(nr):
        k = hop(i, nr - d)
        if d:
            remote(cbuf.at[k], cbuf.at[k], cs.at[k], cr.at[k], at(k, z, q)).wait_recv()

        @pl.when(k == z)
        def _():
            tbuf[z] = cbuf[z]

        @pl.when(k != z)
        def _():
            remote(cbuf.at[k], tbuf.at[z], c2s.at[k], c2r.at[z], at(i, k, q)).start()

    for d in range(nr):
        k = hop(i, nr - d)
        if d:
            remote(zbuf.at[k], gbuf.at[q, k], b2s.at[k], b2r.at[k], at(k, z, q)).wait_recv()
        send(gbuf.at[q, k], gbuf.at[q, k], b3s.at[0, k], b3r.at[0, k], at(i, z, far))
        send(gbuf.at[q, k], gbuf.at[q, k], b3s.at[1, k], b3r.at[1, k], at(i, z, twin))
    for d in range(nr):
        k = hop(i, nr - d)
        remote(gbuf.at[far, k], gbuf.at[far, k], b3s.at[0, k], b3r.at[0, k], at(i, z, far)).wait_recv()
        send(gbuf.at[far, k], gbuf.at[far, k], b3s.at[2, k], b3r.at[2, k], at(i, z, twin))

    for e in range(1, ny):
        k = xl * ny + (y + ny - e) % ny
        remote(abuf.at[k], abuf.at[k], asnd.at[e], arcv.at[e], at(k, z, q)).wait_recv()
    for e in range(1, ny):
        k = (1 - xl) * ny + (y + ny - e) % ny
        remote(abuf.at[k], abuf.at[k], afs.at[e], afr.at[e], at(k, z, q)).wait_recv()

    @pl.loop(0, nr)
    def _(k):
        keys = abuf[k, pl.ds(PAIRS_A * BS, KEYS)].astype(F32)
        for u in range(PAIRS_A):
            block = abuf[k, pl.ds(u * BS, BS)]
            for r in range(FB_DEV):
                mask = tile_rows((keys[u : u + 1] == r).astype(F32))
                left[k, pl.ds(r * BS, BS), pl.ds(u * LANES, LANES)] = scaled(block, mask)

    for d in range(1, nr):
        k = hop(z, d)
        remote(cbuf.at[k], tbuf.at[k], c2s.at[k], c2r.at[k], at(i, k, q)).wait_recv()

    def sources(tile):
        keys = tile[PAIRS_P * BS :].astype(F32)
        found = []
        for u in range(PAIRS_P):
            block = tile[u * BS : (u + 1) * BS]
            key = keys[u : u + 1]
            found += [(block, key), (swap_halves(block), swap_halves(key))]
        return found

    half_f = half.astype(F32)

    @pl.loop(0, nr)
    def _(k):
        found = sources(tbuf[k])
        for c in range(0, Q * FB_DEV, 2):
            strip = []
            for cc in (c, c + 1):
                total = jnp.zeros((BS, LANES), BF16)
                for block, key in found:
                    total += scaled(block, tile_rows((key == 2 * cc + half_f).astype(F32)))
                strip.append(total)
            square = jnp.concatenate(strip, axis=0).astype(F32)
            restrict[k, :, pl.ds(c * BS, LANES)] = square.T.astype(BF16)

    def multiply(first):
        acc[...] = jnp.zeros_like(acc)

        @pl.loop(0, nr)
        def _(k):
            cols = abuf[k, pl.ds(PAIRS_A * BS + KEYS, SLOTS_A)].astype(F32)
            for w in range(2):
                found = sources(gbuf[first + w, k])
                masks = [(cols == key).astype(F32) for _, key in found]
                for s in range(SLOTS_A):
                    total = jnp.zeros((BS, LANES), BF16)
                    for (block, _), mask in zip(found, masks):
                        total += scaled(block, tile_rows(mask[s : s + 1]))
                    rhs[pl.ds(s * BS, BS), pl.ds(w * LANES, LANES)] = total
            acc[...] += jnp.dot(left[k], rhs[...], preferred_element_type=F32)

    for h in range(2):
        side = q // 2 if h == 0 else 1 - q // 2
        for d in range(nr):
            k = hop(i, nr - d)
            if h == 0:
                remote(gbuf.at[twin, k], gbuf.at[twin, k], b3s.at[1, k], b3r.at[1, k], at(i, z, twin)).wait_recv()
            else:
                remote(
                    gbuf.at[far_twin, k], gbuf.at[far_twin, k], b3s.at[2, k], b3r.at[2, k], at(i, z, twin)
                ).wait_recv()
        multiply(2 * side)
        prod[q, side] = acc[...].astype(BF16)
        send(prod.at[q, side], prod.at[q, side], pgs.at[0, h], pgr.at[0, h], at(i, z, far))
        send(prod.at[q, side], prod.at[q, side], pgs.at[1, h], pgr.at[1, h], at(i, z, twin))
    for h in range(2):
        side = 1 - q // 2 if h == 0 else q // 2
        remote(prod.at[far, side], prod.at[far, side], pgs.at[0, h], pgr.at[0, h], at(i, z, far)).wait_recv()
        send(prod.at[far, side], prod.at[far, side], pgs.at[2, h], pgr.at[2, h], at(i, z, twin))
    for h in range(2):
        side = q // 2 if h == 0 else 1 - q // 2
        remote(prod.at[twin, side], prod.at[twin, side], pgs.at[1, h], pgr.at[1, h], at(i, z, twin)).wait_recv()
        remote(
            prod.at[far_twin, 1 - side], prod.at[far_twin, 1 - side], pgs.at[2, h], pgr.at[2, h], at(i, z, twin)
        ).wait_recv()

    def share(k, h):
        total = jnp.zeros((LANES, HALF), F32)
        for p in range(Q):
            total += jnp.dot(
                restrict[k, :, p * FINE : (p + 1) * FINE], prod[p, h], preferred_element_type=F32
            )
        return total

    order = sorted(range(1, nr), key=lambda d: -min(d, nr - d))
    for d in order:
        k = hop(z, d)

        @pl.loop(0, 2)
        def _(h):
            outgoing[k, h] = share(k, h).astype(BF16)

        send(outgoing.at[k], incoming.at[z], fs.at[k], fr.at[z], at(i, k, q))

    @pl.loop(0, 2)
    def _(h):
        own[h] = share(z, h)

    for d in reversed(order):
        k = hop(z, d)
        remote(outgoing.at[k], incoming.at[k], fs.at[k], fr.at[k], at(i, k, q)).wait_recv()
    for h in range(2):
        total = own[h]
        for d in range(1, nr):
            total += incoming[hop(z, d), h].astype(F32)
        out_ref[:, h * HALF : (h + 1) * HALF] = total

    for copy in sent:
        copy.wait_send()
    for k in range(nr):

        @pl.when(k != i)
        def _():
            remote(zbuf.at[k], gbuf.at[q, i], b2s.at[k], b2r.at[i], at(k, z, q)).wait_send()

        @pl.when(k != z)
        def _():
            remote(cbuf.at[k], tbuf.at[z], c2s.at[k], c2r.at[z], at(i, k, q)).wait_send()


def pairs(values, slots):
    blocks = values.reshape(slots // 2, 2, BS, BS)
    return blocks.transpose(0, 2, 1, 3).reshape(slots // 2 * BS, LANES)


def solution(mesh):
    nr = mesh.shape["row"]
    ny = nr // 2

    def shards(a_values, a_rows, a_cols, a_count, p_values, p_rows, p_cols, p_count):
        dma = lambda *n: pltpu.SemaphoreType.DMA(n)
        smem = pl.BlockSpec(memory_space=pltpu.SMEM)
        vmem = pl.BlockSpec(memory_space=pltpu.VMEM)
        lists = lambda n=1: pltpu.VMEM((n, nr, P_ROWS, LANES), BF16)
        return pl.pallas_call(
            functools.partial(kernel, nr),
            out_shape=jax.ShapeDtypeStruct((CB_DEV * BS, 2 * HALF), F32),
            in_specs=[smem] * 6 + [vmem] * 2,
            out_specs=vmem,
            scratch_shapes=[
                pltpu.VMEM((nr, A_ROWS, LANES), BF16),
                pltpu.VMEM((nr, P_ROWS, LANES), BF16),
                pltpu.VMEM((nr, P_ROWS, LANES), BF16),
                pltpu.VMEM((nr, P_ROWS, LANES), BF16),
                pltpu.VMEM((Q, nr, P_ROWS, LANES), BF16),
                pltpu.VMEM((nr, FINE, SLOTS_A * BS), BF16),
                pltpu.VMEM((SLOTS_A * BS, HALF), BF16),
                pltpu.VMEM((nr, LANES, Q * FINE), BF16),
                pltpu.VMEM((FINE, HALF), F32),
                pltpu.VMEM((Q, 2, FINE, HALF), BF16),
                pltpu.VMEM((nr, 2, LANES, HALF), BF16),
                pltpu.VMEM((nr, 2, LANES, HALF), BF16),
                pltpu.VMEM((2, LANES, HALF), F32),
                dma(nr), dma(nr), dma(nr), dma(nr),
                dma(ny), dma(ny), dma(ny), dma(ny),
                dma(nr), dma(nr), dma(nr), dma(nr),
                dma(3, nr), dma(3, nr),
                dma(3, 2), dma(3, 2),
                dma(nr), dma(nr),
            ],
            compiler_params=pltpu.CompilerParams(
                collective_id=0, has_side_effects=True, vmem_limit_bytes=40 * 2**20
            ),
        )(
            a_rows, a_cols, a_count, p_rows, p_cols, p_count,
            pairs(a_values[0], SLOTS_A), pairs(p_values[0], SLOTS_P),
        )

    return jax.shard_map(
        shards,
        mesh=mesh,
        in_specs=(
            P("col", "row", None),
            P("col", "row"),
            P("col", "row"),
            P("col", "row"),
            P("row", "col", None),
            P("row", "col"),
            P("row", "col"),
            P("row", "col"),
        ),
        out_specs=P("col", "row"),
        check_vma=False,
    )
```

time: 427 us -> 84.4 us (0.20)
  the two profiles are of different devices: /device:TPU:4 before, /device:TPU:1 now
where the time goes in v1:
time: 84.4 us; the launch traced here: 84.2 us
  Pallas kernels  79.6 us (94%)
  local copies, waits for them, and re-layouts  3.21 us (4%)
  between operations  1.43 us (2%)
    pallas_call x1, Pallas kernels, shards(): pl.pallas_call(functools.partial(kernel, nr), out_shape=jax.ShapeDtypeStr...  79.6 us

profile of v1, /device:TPU:1, one launch (start us, length us, event | category | flops | bytes accessed | tf_op | source)
XLA Modules:
  0.0 84.2 jit_solution(194244379468058739)
XLA Ops:
  0.0 1.2 %reshape_squeeze.6 = bf16[8,2,64,64]{3,2,1,0:T(8,128)(2,1)S(1)} reshape(bf16[1,16,4096]{2,1,0:T(8,128)(2,1)} %param.8) | data formatting | bytes 262144 | tf_op jit(solution)/shard_map/reshape;squeeze | solution.py:289
  1.2 0.3 copy.13
  1.5 0.0 copy-start.4
  1.5 0.1 reshape.6.a_ref
  1.6 0.6 copy-done.4
  2.2 0.1 reshape_squeeze.7
  2.3 0.1 copy.14
  2.4 0.0 copy-start.3
  2.4 0.1 reshape.7.p_ref
  3.2 0.0 copy-start
  3.2 0.0 copy-start.1
  3.2 0.0 copy-start.2
  3.9 0.0 copy-done.3
  3.9 0.0 copy-done
  3.9 0.0 copy-done.1
  3.9 0.0 copy-done.2
  3.9 79.6 %shard_map.82 = f32[128,512]{1,0:T(8,128)S(1)} custom-call(s32[1,16]{1,0:T(1,128)S(1)} %copy-done, s32[1,16]{1,0:T(1,128)S(1)} %copy-done.1, s32[1,1]{1,0:T(1,128)S(6)} %copy.16.an, s32[1,4]{1,0:T(1,128)S(1)} %copy-done.2, s32[1,4]{1,0:T(1,128)S(1)} %copy-done.3, s32[1,1]{1,0:T(1,128)S(6)} %copy.17.pn, bf16[512,128]{1,0:T(8,128)(2,1)S(1)} %reshape.6.a_ref, ...), custom_call_target="tpu_custom_call" | custom-call | tf_op jit(solution)/shard_map/pallas_call | solution.py:302
  83.5 0.7 copy.18
Async XLA Ops:
  1.5 0.8 copy-start.4
  2.4 1.5 %copy-start.3 = (s32[1,4]{1,0:T(1,128)S(1)}, s32[1,4]{1,0:T(1,128)}, u32[]{:S(2)}) copy-start(s32[1,4]{1,0:T(1,128)} %pc.1) | copy-start | bytes 52
  3.2 0.7 copy-start
  3.2 0.7 copy-start.1
  3.2 0.7 copy-start.2

commit v2 on v1

--- a/solution.py
+++ b/solution.py
@@ -47,8 +47,8 @@
 def kernel(
     nr,
     ar, ac, an, pr, pc, pn, a_ref, p_ref, out_ref,
-    abuf, zbuf, cbuf, tbuf, gbuf, left, rhs, restrict, acc, prod, outgoing, incoming, own,
-    zs, zr, cs, cr, asnd, arcv, afs, afr, b2s, b2r, c2s, c2r, b3s, b3r, pgs, pgr, fs, fr,
+    flat, woven, abuf, zbuf, cbuf, tbuf, gbuf, left, rhs, restrict, acc, prod, outgoing, incoming, own_out, own_in, own,
+    zs, zr, cs, cr, asnd, arcv, afs, afr, b2s, b2r, c2s, c2r, b3s, b3r, pgs, pgr, fs, fr, os, orc,
 ):
     ny = nr // 2
     i = lax.axis_index("row")
@@ -56,6 +56,8 @@
     z, q = j // Q, j % Q
     xl, y = i // ny, i % ny
     mate = (1 - xl) * ny + y
+    upper = q // 2 == 1
+    row_of = lambda k: jnp.where(upper, (k + ny) % nr, k)
     twin = q + 1 - 2 * (q % 2)
     far = (q + 2) % Q
     far_twin = (twin + 2) % Q
@@ -67,10 +69,22 @@
         pl.semaphore_signal(barrier, inc=1, device_id=at(hop(i, d), z, q), device_id_type=MESH)
         pl.semaphore_signal(barrier, inc=1, device_id=at(i, hop(z, d), q), device_id_type=MESH)
     pl.semaphore_signal(barrier, inc=1, device_id=at(i, z, twin), device_id_type=MESH)
-    pl.semaphore_signal(barrier, inc=1, device_id=at(i, z, far), device_id_type=MESH)
+    pl.semaphore_signal(barrier, inc=1, device_id=at(mate, z, far), device_id_type=MESH)
+    for d in {1, nr - 1}:
+        pl.semaphore_signal(barrier, inc=1, device_id=at(mate, hop(z, d), q), device_id_type=MESH)
 
     lane = lax.broadcasted_iota(jnp.int32, (1, LANES), 1)
     second = lane >= BS
+    def pack(ref, slots):
+        for m in range(BS // 2):
+            flat[pl.ds(m, slots, stride=BS // 2)] = ref[0, :, m * LANES : (m + 1) * LANES].astype(F32)
+        for u in range(slots // 2):
+            one = flat[pl.ds(u * BS, BS // 2)]
+            two = flat[pl.ds(u * BS + BS // 2, BS // 2)]
+            woven[pl.ds(u * BS, BS // 2, stride=2)] = jnp.where(second, swap_halves(two), one)
+            woven[pl.ds(u * BS + 1, BS // 2, stride=2)] = jnp.where(second, two, swap_halves(one))
+        return woven[pl.ds(0, slots // 2 * BS)].astype(BF16)
+
     half = second.astype(jnp.int32)
     rows_u = lax.broadcasted_iota(jnp.int32, (KEYS, LANES), 0)
     rows_s = lax.broadcasted_iota(jnp.int32, (SLOTS_A, LANES), 0)
@@ -81,7 +95,7 @@
             jnp.where(s < pn[0, 0], pr[0, s] * CB_DEV + pc[0, s], -1) for s in (2 * u, 2 * u + 1)
         ]
         p_keys = jnp.where(rows_u == u, jnp.where(second, keys[1], keys[0]), p_keys)
-    tile = jnp.concatenate([p_ref[...], p_keys.astype(F32).astype(BF16)], axis=0)
+    tile = jnp.concatenate([pack(p_ref, SLOTS_P), p_keys.astype(F32).astype(BF16)], axis=0)
     zbuf[z] = tile
     cbuf[i] = tile
     a_keys = jnp.full((KEYS, LANES), -1, jnp.int32)
@@ -93,10 +107,10 @@
         a_cols = jnp.where(rows_s == s, ac[0, s], a_cols)
     a_cols = a_cols * 2 + half_s
     abuf[i] = jnp.concatenate(
-        [a_ref[...], a_keys.astype(F32).astype(BF16), a_cols.astype(F32).astype(BF16)], axis=0
+        [pack(a_ref, SLOTS_A), a_keys.astype(F32).astype(BF16), a_cols.astype(F32).astype(BF16)], axis=0
     )
 
-    pl.semaphore_wait(barrier, 2 * (nr - 1) + 2)
+    pl.semaphore_wait(barrier, 2 * (nr - 1) + 2 + len({1, nr - 1}))
 
     sent = []
 
@@ -120,13 +134,15 @@
         if d:
             remote(zbuf.at[k], zbuf.at[k], zs.at[k], zr.at[k], at(i, k, q)).wait_recv()
 
-        @pl.when(k == i)
-        def _():
-            gbuf[q, i] = zbuf[i]
-
-        @pl.when(k != i)
-        def _():
-            remote(zbuf.at[k], gbuf.at[q, i], b2s.at[k], b2r.at[i], at(k, z, q)).start()
+        to = row_of(k)
+
+        @pl.when(to == i)
+        def _():
+            gbuf[q, i] = zbuf[k]
+
+        @pl.when(to != i)
+        def _():
+            remote(zbuf.at[k], gbuf.at[q, i], b2s.at[k], b2r.at[i], at(to, z, q)).start()
 
     remote(abuf.at[mate], abuf.at[mate], asnd.at[0], arcv.at[0], at(mate, z, q)).wait_recv()
     for e in range(1, ny):
@@ -149,13 +165,8 @@
         k = hop(i, nr - d)
         if d:
             remote(zbuf.at[k], gbuf.at[q, k], b2s.at[k], b2r.at[k], at(k, z, q)).wait_recv()
-        send(gbuf.at[q, k], gbuf.at[q, k], b3s.at[0, k], b3r.at[0, k], at(i, z, far))
+        send(gbuf.at[q, k], gbuf.at[q, k], b3s.at[0, k], b3r.at[0, k], at(mate, z, far))
         send(gbuf.at[q, k], gbuf.at[q, k], b3s.at[1, k], b3r.at[1, k], at(i, z, twin))
-    for d in range(nr):
-        k = hop(i, nr - d)
-        remote(gbuf.at[far, k], gbuf.at[far, k], b3s.at[0, k], b3r.at[0, k], at(i, z, far)).wait_recv()
-        send(gbuf.at[far, k], gbuf.at[far, k], b3s.at[2, k], b3r.at[2, k], at(i, z, twin))
-
     for e in range(1, ny):
         k = xl * ny + (y + ny - e) % ny
         remote(abuf.at[k], abuf.at[k], asnd.at[e], arcv.at[e], at(k, z, q)).wait_recv()
@@ -200,39 +211,41 @@
             square = jnp.concatenate(strip, axis=0).astype(F32)
             restrict[k, :, pl.ds(c * BS, LANES)] = square.T.astype(BF16)
 
-    def multiply(first):
-        acc[...] = jnp.zeros_like(acc)
-
-        @pl.loop(0, nr)
-        def _(k):
-            cols = abuf[k, pl.ds(PAIRS_A * BS + KEYS, SLOTS_A)].astype(F32)
-            for w in range(2):
-                found = sources(gbuf[first + w, k])
-                masks = [(cols == key).astype(F32) for _, key in found]
-                for s in range(SLOTS_A):
-                    total = jnp.zeros((BS, LANES), BF16)
-                    for (block, _), mask in zip(found, masks):
-                        total += scaled(block, tile_rows(mask[s : s + 1]))
-                    rhs[pl.ds(s * BS, BS), pl.ds(w * LANES, LANES)] = total
-            acc[...] += jnp.dot(left[k], rhs[...], preferred_element_type=F32)
-
+    def multiply(first, k):
+        cols = abuf[k, pl.ds(PAIRS_A * BS + KEYS, SLOTS_A)].astype(F32)
+        for w in range(2):
+            found = sources(gbuf[first + w, k])
+            masks = [(cols == key).astype(F32) for _, key in found]
+            for s in range(SLOTS_A):
+                total = jnp.zeros((BS, LANES), BF16)
+                for (block, _), mask in zip(found, masks):
+                    total += scaled(block, tile_rows(mask[s : s + 1]))
+                rhs[pl.ds(s * BS, BS), pl.ds(w * LANES, LANES)] = total
+        acc[...] += jnp.dot(left[k], rhs[...], preferred_element_type=F32)
+
+    from_far = lambda k: remote(gbuf.at[far, k], gbuf.at[far, k], b3s.at[0, k], b3r.at[0, k], at(mate, z, far))
+    from_twin = lambda p, s, k: remote(gbuf.at[p, k], gbuf.at[p, k], b3s.at[s, k], b3r.at[s, k], at(i, z, twin))
     for h in range(2):
         side = q // 2 if h == 0 else 1 - q // 2
-        for d in range(nr):
+        acc[...] = jnp.zeros_like(acc)
+
+        @pl.loop(0, nr)
+        def _(d):
             k = hop(i, nr - d)
             if h == 0:
-                remote(gbuf.at[twin, k], gbuf.at[twin, k], b3s.at[1, k], b3r.at[1, k], at(i, z, twin)).wait_recv()
+                from_far(k).wait_recv()
+                from_twin(far, 2, k).start()
+                from_twin(twin, 1, k).wait_recv()
             else:
-                remote(
-                    gbuf.at[far_twin, k], gbuf.at[far_twin, k], b3s.at[2, k], b3r.at[2, k], at(i, z, twin)
-                ).wait_recv()
-        multiply(2 * side)
+                from_twin(far_twin, 2, k).wait_recv()
+            multiply(2 * side, k)
+
         prod[q, side] = acc[...].astype(BF16)
-        send(prod.at[q, side], prod.at[q, side], pgs.at[0, h], pgr.at[0, h], at(i, z, far))
+        send(prod.at[q, side], prod.at[q, side], pgs.at[0, h], pgr.at[0, h], at(mate, z, far))
         send(prod.at[q, side], prod.at[q, side], pgs.at[1, h], pgr.at[1, h], at(i, z, twin))
     for h in range(2):
         side = 1 - q // 2 if h == 0 else q // 2
-        remote(prod.at[far, side], prod.at[far, side], pgs.at[0, h], pgr.at[0, h], at(i, z, far)).wait_recv()
+        remote(prod.at[far, side], prod.at[far, side], pgs.at[0, h], pgr.at[0, h], at(mate, z, far)).wait_recv()
         send(prod.at[far, side], prod.at[far, side], pgs.at[2, h], pgr.at[2, h], at(i, z, twin))
     for h in range(2):
         side = q // 2 if h == 0 else 1 - q // 2
@@ -249,45 +262,64 @@
             )
         return total
 
-    order = sorted(range(1, nr), key=lambda d: -min(d, nr - d))
-    for d in order:
-        k = hop(z, d)
-
-        @pl.loop(0, 2)
-        def _(h):
-            outgoing[k, h] = share(k, h).astype(BF16)
-
-        send(outgoing.at[k], incoming.at[z], fs.at[k], fr.at[z], at(i, k, q))
-
-    @pl.loop(0, 2)
-    def _(h):
-        own[h] = share(z, h)
-
-    for d in reversed(order):
-        k = hop(z, d)
-        remote(outgoing.at[k], incoming.at[k], fs.at[k], fr.at[k], at(i, k, q)).wait_recv()
+    half_way = nr // 2
+    home = row_of(i)
+
+    def leg(way, t, h):
+        to = hop(z, 1 if way == 0 else nr - 1)
+        row = home if t == half_way - 1 else i
+        return remote(outgoing.at[way, t, h], incoming.at[way, t, h], fs.at[way, t, h], fr.at[way, t, h], at(row, to, q))
+
+    for t in range(half_way):
+        for other in (True, False):
+            for way in range(2):
+                h = 1 - way if other else way
+                if t == 0 and other:
+                    continue
+                far_z = hop(z, half_way - t if way == 0 else nr - half_way + t)
+                total = share(far_z, h)
+                if t > 1 or (t == 1 and not other):
+                    leg(way, t - 1, h).wait_recv()
+                    total += incoming[way, t - 1, h].astype(F32)
+                outgoing[way, t, h] = total.astype(BF16)
+                copy = leg(way, t, h)
+                copy.start()
+                sent.append(copy)
+        if t == 0:
+            for h in range(2):
+                own[h] = share(z, h)
+
+            @pl.when(upper)
+            def _():
+                own_out[...] = own[...].astype(BF16)
+                remote(own_out, own_in, os, orc, at(mate, z, q)).start()
+
+    @pl.when(upper)
+    def _():
+        remote(own_out, own_in, os, orc, at(mate, z, q)).wait()
+        own[...] = own_in[...].astype(F32)
+
     for h in range(2):
         total = own[h]
-        for d in range(1, nr):
-            total += incoming[hop(z, d), h].astype(F32)
+        for way in range(2):
+            if half_way == 1 and h != way:
+                continue
+            leg(way, half_way - 1, h).wait_recv()
+            total += incoming[way, half_way - 1, h].astype(F32)
         out_ref[:, h * HALF : (h + 1) * HALF] = total
 
     for copy in sent:
         copy.wait_send()
     for k in range(nr):
-
-        @pl.when(k != i)
-        def _():
-            remote(zbuf.at[k], gbuf.at[q, i], b2s.at[k], b2r.at[i], at(k, z, q)).wait_send()
+        from_twin(far, 2, k).wait_send()
+
+        @pl.when(row_of(k) != i)
+        def _():
+            remote(zbuf.at[k], gbuf.at[q, i], b2s.at[k], b2r.at[i], at(row_of(k), z, q)).wait_send()
 
         @pl.when(k != z)
         def _():
             remote(cbuf.at[k], tbuf.at[z], c2s.at[k], c2r.at[z], at(i, k, q)).wait_send()
-
-
-def pairs(values, slots):
-    blocks = values.reshape(slots // 2, 2, BS, BS)
-    return blocks.transpose(0, 2, 1, 3).reshape(slots // 2 * BS, LANES)
 
 
 def solution(mesh):
@@ -305,6 +337,8 @@
             in_specs=[smem] * 6 + [vmem] * 2,
             out_specs=vmem,
             scratch_shapes=[
+                pltpu.VMEM((SLOTS_A * BS // 2, LANES), F32),
+                pltpu.VMEM((SLOTS_A * BS // 2, LANES), F32),
                 pltpu.VMEM((nr, A_ROWS, LANES), BF16),
                 pltpu.VMEM((nr, P_ROWS, LANES), BF16),
                 pltpu.VMEM((nr, P_ROWS, LANES), BF16),
@@ -315,22 +349,25 @@
                 pltpu.VMEM((nr, LANES, Q * FINE), BF16),
                 pltpu.VMEM((FINE, HALF), F32),
                 pltpu.VMEM((Q, 2, FINE, HALF), BF16),
-                pltpu.VMEM((nr, 2, LANES, HALF), BF16),
-                pltpu.VMEM((nr, 2, LANES, HALF), BF16),
+                pltpu.VMEM((2, ny, 2, LANES, HALF), BF16),
+                pltpu.VMEM((2, ny, 2, LANES, HALF), BF16),
+                pltpu.VMEM((2, LANES, HALF), BF16),
+                pltpu.VMEM((2, LANES, HALF), BF16),
                 pltpu.VMEM((2, LANES, HALF), F32),
                 dma(nr), dma(nr), dma(nr), dma(nr),
                 dma(ny), dma(ny), dma(ny), dma(ny),
                 dma(nr), dma(nr), dma(nr), dma(nr),
                 dma(3, nr), dma(3, nr),
                 dma(3, 2), dma(3, 2),
-                dma(nr), dma(nr),
+                dma(2, ny, 2), dma(2, ny, 2),
+                pltpu.SemaphoreType.DMA, pltpu.SemaphoreType.DMA,
             ],
             compiler_params=pltpu.CompilerParams(
                 collective_id=0, has_side_effects=True, vmem_limit_bytes=40 * 2**20
             ),
         )(
             a_rows, a_cols, a_count, p_rows, p_cols, p_count,
-            pairs(a_values[0], SLOTS_A), pairs(p_values[0], SLOTS_P),
+            a_values, p_values,
         )
 
     return jax.shard_map(

time: 84.4 us -> 73.6 us (0.87)
  the two profiles are of different devices: /device:TPU:1 before, /device:TPU:4 now
where the time goes in v2:
time: 73.6 us; the launch traced here: 73.4 us
  Pallas kernels  69.6 us (95%)
  local copies, waits for them, and re-layouts  2.38 us (3%)
  between operations  1.41 us (2%)
    pallas_call x1, Pallas kernels, shards(): pl.pallas_call(functools.partial(kernel, nr), out_shape=jax.ShapeDtypeStr...  69.6 us
    unnamed x13, local copies, waits for them, and re-layouts  2.38 us

profile of v2, /device:TPU:4, one launch (start us, length us, event | category | flops | bytes accessed | tf_op | source)
XLA Modules:
  0.0 73.4 jit_solution(2591982899882957948)
XLA Ops:
  0.0 0.0 copy-start.5
  0.7 0.0 copy-start.2
  0.7 0.0 copy-start.3
  0.7 0.0 copy-start.4
  1.4 0.0 copy-done.5
  1.4 0.0 copy-done.2
  1.4 0.0 copy-done.3
  1.4 0.0 copy-done.4
  1.4 0.0 copy-start
  1.4 0.9 %copy-done = bf16[1,16,4096]{2,1,0:T(8,128)(2,1)S(1)} copy-done((bf16[1,16,4096]{2,1,0:T(8,128)(2,1)S(1)}, bf16[1,16,4096]{2,1,0:T(8,128)(2,1)}, u32[]{:S(2)}) %copy-start) | copy-done | bytes 131096
  2.3 0.0 copy-start.1
  2.3 0.8 %copy-done.1 = bf16[1,4,4096]{2,1,0:T(4,128)(2,1)S(1)} copy-done((bf16[1,4,4096]{2,1,0:T(4,128)(2,1)S(1)}, bf16[1,4,4096]{2,1,0:T(4,128)(2,1)}, u32[]{:S(2)}) %copy-start.1) | copy-done | bytes 32792
  3.1 69.6 %shard_map.82 = f32[128,512]{1,0:T(8,128)S(1)} custom-call(s32[1,16]{1,0:T(1,128)S(1)} %copy-done.2, s32[1,16]{1,0:T(1,128)S(1)} %copy-done.3, s32[1,1]{1,0:T(1,128)S(6)} %copy.10.an, s32[1,4]{1,0:T(1,128)S(1)} %copy-done.4, s32[1,4]{1,0:T(1,128)S(1)} %copy-done.5, s32[1,1]{1,0:T(1,128)S(6)} %copy.11.pn, bf16[1,16,4096]{2,1,0:T(8,128)(2,1)S(1)} %copy-done, ...), custom_call_target="tpu_custom_call" | custom-call | tf_op jit(solution)/shard_map/pallas_call | solution.py:334
  72.7 0.7 copy.12
Async XLA Ops:
  0.0 1.4 %copy-start.5 = (s32[1,4]{1,0:T(1,128)S(1)}, s32[1,4]{1,0:T(1,128)}, u32[]{:S(2)}) copy-start(s32[1,4]{1,0:T(1,128)} %pc.1) | copy-start | bytes 52
  0.7 0.7 copy-start.2
  0.7 0.7 copy-start.3
  0.7 0.7 copy-start.4
  1.4 0.9 %copy-start = (bf16[1,16,4096]{2,1,0:T(8,128)(2,1)S(1)}, bf16[1,16,4096]{2,1,0:T(8,128)(2,1)}, u32[]{:S(2)}) copy-start(bf16[1,16,4096]{2,1,0:T(8,128)(2,1)} %a_ref.1) | copy-start | bytes 393220
  2.3 0.8 %copy-start.1 = (bf16[1,4,4096]{2,1,0:T(4,128)(2,1)S(1)}, bf16[1,4,4096]{2,1,0:T(4,128)(2,1)}, u32[]{:S(2)}) copy-start(bf16[1,4,4096]{2,1,0:T(4,128)(2,1)} %p_ref.1) | copy-start | bytes 98308

commit v3 on v2

v3 whole, which is shorter than its diff:
```python
import functools

import jax
import jax.numpy as jnp
from jax import lax
from jax.experimental import pallas as pl
from jax.experimental.pallas import tpu as pltpu
from jax.sharding import PartitionSpec as P

BS = 64
FB_DEV = 4
CB_DEV = 2
Q = 4
SLOTS_A = 16
SLOTS_P = 4
PAIRS_A = SLOTS_A // 2
PAIRS_P = SLOTS_P // 2
LANES = 2 * BS
KEYS = 16
A_ROWS = PAIRS_A * BS + KEYS + SLOTS_A
P_ROWS = PAIRS_P * BS + KEYS
FINE = FB_DEV * BS
HALF = 2 * CB_DEV * BS
MESH = pl.DeviceIdType.MESH
BF16 = jnp.bfloat16
F32 = jnp.float32


def remote(src, dst, send, recv, target):
    return pltpu.make_async_remote_copy(
        src_ref=src, dst_ref=dst, send_sem=send, recv_sem=recv, device_id=target, device_id_type=MESH
    )


def swap_halves(x):
    return jnp.concatenate([x[:, BS:], x[:, :BS]], axis=1)


def spread(row):
    return jnp.broadcast_to(row, (BS, LANES)).astype(BF16)


def kernel(
    nr,
    ar_h, ac_h, an_h, pr_h, pc_h, pn_h, a_h, p_h, out_ref,
    ar, ac, an, pr, pc, pn, a_ref, p_ref, flat, woven, abuf, cbuf, tbuf, gbuf, left, rhs0, rhs1, restrict, acc, prod, outgoing, incoming, own_out, own_in, own,
    ins, zs, zr, cs, cr, asnd, arcv, ans, anr, afs, afr, c2s, c2r, b3s, b3r, pgs, pgr, fs, fr, os, orc,
):
    ny = nr // 2
    i = lax.axis_index("row")
    j = lax.axis_index("col")
    z, q = j // Q, j % Q
    xl, y = i // ny, i % ny
    mate = (1 - xl) * ny + y
    upper = q // 2 == 1
    row_of = lambda k: jnp.where(upper, (k + ny) % nr, k)
    twin = q + 1 - 2 * (q % 2)
    far = (q + 2) % Q
    far_twin = (twin + 2) % Q
    at = lambda row, zz, qq: (row, zz * Q + qq)
    hop = lambda k, d: (k + d) % nr

    barrier = pltpu.get_barrier_semaphore()
    for d in range(1, nr):
        pl.semaphore_signal(barrier, inc=1, device_id=at(hop(i, d), z, q), device_id_type=MESH)
        pl.semaphore_signal(barrier, inc=1, device_id=at(i, hop(z, d), q), device_id_type=MESH)
        pl.semaphore_signal(barrier, inc=1, device_id=at(hop(i, d), row_of(i), q), device_id_type=MESH)
    pl.semaphore_signal(barrier, inc=1, device_id=at(i, z, twin), device_id_type=MESH)
    pl.semaphore_signal(barrier, inc=1, device_id=at(mate, z, far), device_id_type=MESH)

    @pl.when(row_of(i) != z)
    def _():
        pl.semaphore_signal(barrier, inc=1, device_id=at(i, row_of(i), q), device_id_type=MESH)

    for d in {1, nr - 1}:
        pl.semaphore_signal(barrier, inc=1, device_id=at(mate, hop(z, d), q), device_id_type=MESH)

    loads = [
        pltpu.make_async_copy(src, dst, ins.at[n])
        for n, (src, dst) in enumerate(
            [(p_h, p_ref), (pr_h, pr), (pc_h, pc), (pn_h, pn), (a_h, a_ref), (ar_h, ar), (ac_h, ac), (an_h, an)]
        )
    ]
    for load in loads:
        load.start()

    lane = lax.broadcasted_iota(jnp.int32, (1, LANES), 1)
    second = lane >= BS

    def pack(ref, slots):
        for m in range(BS // 2):
            flat[pl.ds(m, slots, stride=BS // 2)] = ref[0, :, m * LANES : (m + 1) * LANES].astype(F32)
        for u in range(slots // 2):
            one = flat[pl.ds(u * BS, BS // 2)]
            two = flat[pl.ds(u * BS + BS // 2, BS // 2)]
            woven[pl.ds(u * BS, BS // 2, stride=2)] = jnp.where(second, swap_halves(two), one)
            woven[pl.ds(u * BS + 1, BS // 2, stride=2)] = jnp.where(second, two, swap_halves(one))
        return woven[pl.ds(0, slots // 2 * BS)].astype(BF16)

    half = second.astype(jnp.int32)
    rows_u = lax.broadcasted_iota(jnp.int32, (KEYS, LANES), 0)
    rows_s = lax.broadcasted_iota(jnp.int32, (SLOTS_A, LANES), 0)
    half_s = (lax.broadcasted_iota(jnp.int32, (SLOTS_A, LANES), 1) >= BS).astype(jnp.int32)
    for load in loads[:4]:
        load.wait()
    p_keys = jnp.full((KEYS, LANES), -1, jnp.int32)
    for u in range(PAIRS_P):
        keys = [
            jnp.where(s < pn[0, 0], pr[0, s] * CB_DEV + pc[0, s], -1) for s in (2 * u, 2 * u + 1)
        ]
        p_keys = jnp.where(rows_u == u, jnp.where(second, keys[1], keys[0]), p_keys)
    tile = jnp.concatenate([pack(p_ref, SLOTS_P), p_keys.astype(F32).astype(BF16)], axis=0)
    cbuf[i] = tile
    for load in loads[4:]:
        load.wait()
    a_keys = jnp.full((KEYS, LANES), -1, jnp.int32)
    for u in range(PAIRS_A):
        keys = [jnp.where(s < an[0, 0], ar[0, s], -1) for s in (2 * u, 2 * u + 1)]
        a_keys = jnp.where(rows_u == u, jnp.where(second, keys[1], keys[0]), a_keys)
    a_cols = jnp.zeros((SLOTS_A, LANES), jnp.int32)
    for s in range(SLOTS_A):
        a_cols = jnp.where(rows_s == s, ac[0, s], a_cols)
    a_cols = a_cols * 2 + half_s
    abuf[i] = jnp.concatenate(
        [pack(a_ref, SLOTS_A), a_keys.astype(F32).astype(BF16), a_cols.astype(F32).astype(BF16)], axis=0
    )

    here = row_of(z) == i
    pl.semaphore_wait(barrier, 3 * nr + len({1, nr - 1}) - here.astype(jnp.int32))

    sent = []

    def send(*args):
        copy = remote(*args)
        copy.start()
        sent.append(copy)

    p_copy = lambda d: remote(
        cbuf.at[i], gbuf.at[q, i], zs.at[d], zr.at[i], at(row_of(z), hop(z, d), q)
    )
    away = sorted(range(1, nr), key=lambda d: -min(d, nr - d))
    for d in away:
        p_copy(d).start()

    @pl.when(here)
    def _():
        gbuf[q, i] = cbuf[i]

    @pl.when(jnp.logical_not(here))
    def _():
        p_copy(0).start()

    line = lambda e: xl * ny + (y + e) % ny
    cross = lambda e: (1 - xl) * ny + (y + e) % ny
    opposite = ny // 2
    a_mate = lambda s, k: remote(abuf.at[k], abuf.at[k], asnd.at[s], arcv.at[s], at(mate, z, q))
    a_line = lambda e, k: remote(abuf.at[k], abuf.at[k], ans.at[e], anr.at[e], at(line(e), z, q))
    a_next = lambda e, k: remote(abuf.at[k], abuf.at[k], afs.at[e], afr.at[e], at(line(e), z, q))

    def launch(copy):
        copy.start()
        sent.append(copy)

    launch(a_mate(0, i))
    for e in range(1, ny):
        launch(a_line(e, i))

    for d in range(1, nr):
        to = hop(i, d)
        send(cbuf.at[i], cbuf.at[i], cs.at[to], cr.at[i], at(to, z, q))

    a_mate(0, mate).wait_recv()
    for e in range(1, ny):
        if e != opposite:
            launch(a_next(e, mate))
    if opposite:
        a_line(opposite, line(opposite)).wait_recv()
        launch(a_mate(1, line(opposite)))

    for d in range(nr):
        k = hop(i, nr - d)

        @pl.when(jnp.logical_not((k == i) & here))
        def _():
            remote(cbuf.at[i], gbuf.at[q, k], zs.at[0], zr.at[k], at(k, row_of(i), q)).wait_recv()

        send(gbuf.at[q, k], gbuf.at[q, k], b3s.at[0, k], b3r.at[0, k], at(mate, z, far))
        send(gbuf.at[q, k], gbuf.at[q, k], b3s.at[1, k], b3r.at[1, k], at(i, z, twin))

    def sources(tile):
        keys = tile[PAIRS_P * BS :].astype(F32)
        found = []
        for u in range(PAIRS_P):
            block = tile[u * BS : (u + 1) * BS]
            key = keys[u : u + 1]
            found += [(block, spread(key)), (swap_halves(block), spread(swap_halves(key)))]
        return found

    def pick(found, wanted):
        total = jnp.zeros((BS, LANES), BF16)
        for block, key in found:
            total = jnp.where(key == wanted, block, total)
        return total

    def lay(first, k, rhs):
        cols = abuf[k, pl.ds(PAIRS_A * BS + KEYS, SLOTS_A)].astype(F32)
        for w in range(2):
            found = sources(gbuf[first + w, k])
            for s in range(SLOTS_A):
                rhs[pl.ds(s * BS, BS), pl.ds(w * LANES, LANES)] = pick(found, spread(cols[s : s + 1]))

    from_far = lambda k: remote(gbuf.at[far, k], gbuf.at[far, k], b3s.at[0, k], b3r.at[0, k], at(mate, z, far))
    from_twin = lambda p, s, k: remote(gbuf.at[p, k], gbuf.at[p, k], b3s.at[s, k], b3r.at[s, k], at(i, z, twin))

    def place(k):
        keys = abuf[k, pl.ds(PAIRS_A * BS, KEYS)].astype(F32)
        for u in range(PAIRS_A):
            block = abuf[k, pl.ds(u * BS, BS)]
            key = spread(keys[u : u + 1])
            for r in range(FB_DEV):
                left[k, pl.ds(r * BS, BS), pl.ds(u * LANES, LANES)] = jnp.where(key == r, block, 0).astype(BF16)

    def multiply(side, panels, arrived, fresh):
        for d in range(len(panels) + 1):
            if d < len(panels):
                arrived(panels[d])
                lay(2 * side, panels[d], (rhs0, rhs1)[d % 2])
            if d > 0:
                part = jnp.dot(left[panels[d - 1]], (rhs1, rhs0)[d % 2][...], preferred_element_type=F32)
                acc[...] = part if fresh and d == 1 else acc[...] + part

    def share_out(side, h):
        prod[q, side] = acc[...].astype(BF16)
        send(prod.at[q, side], prod.at[q, side], pgs.at[0, h], pgr.at[0, h], at(mate, z, far))
        send(prod.at[q, side], prod.at[q, side], pgs.at[1, h], pgr.at[1, h], at(i, z, twin))

    side = q // 2
    near = lambda k: from_twin(twin, 1, k).wait_recv()
    ours = [line(e) for e in range(ny)]
    theirs = [cross(e) for e in range(ny)]
    for e in range(1, ny):
        if e != opposite:
            a_line(e, line(e)).wait_recv()
    for k in ours:
        place(k)
    multiply(side, ours, near, True)
    for d in range(nr):
        k = hop(i, nr - d)
        from_far(k).wait_recv()
        from_twin(far, 2, k).start()

    for d in range(nr):
        k = hop(i, nr - d)
        if d:
            remote(cbuf.at[k], cbuf.at[k], cs.at[k], cr.at[k], at(k, z, q)).wait_recv()

        @pl.when(k == z)
        def _():
            tbuf[z] = cbuf[z]

        @pl.when(k != z)
        def _():
            remote(cbuf.at[k], tbuf.at[z], c2s.at[k], c2r.at[z], at(i, k, q)).start()

    for e in range(1, ny):
        if e != opposite:
            a_next(e, cross(e)).wait_recv()
    if opposite:
        a_mate(1, cross(opposite)).wait_recv()
    for k in theirs:
        place(k)
    multiply(side, theirs, near, False)
    share_out(side, 0)
    multiply(1 - side, ours + theirs, lambda k: from_twin(far_twin, 2, k).wait_recv(), True)
    share_out(1 - side, 1)

    for d in range(1, nr):
        k = hop(z, d)
        remote(cbuf.at[k], tbuf.at[k], c2s.at[k], c2r.at[k], at(i, k, q)).wait_recv()

    half_f = half.astype(F32)

    @pl.loop(0, nr)
    def _(k):
        found = sources(tbuf[k])
        for c in range(0, Q * FB_DEV, 2):
            strip = [pick(found, spread(2 * cc + half_f)) for cc in (c, c + 1)]
            square = jnp.concatenate(strip, axis=0).astype(F32)
            restrict[k, :, pl.ds(c * BS, LANES)] = square.T.astype(BF16)

    for h in range(2):
        side = 1 - q // 2 if h == 0 else q // 2
        remote(prod.at[far, side], prod.at[far, side], pgs.at[0, h], pgr.at[0, h], at(mate, z, far)).wait_recv()
        send(prod.at[far, side], prod.at[far, side], pgs.at[2, h], pgr.at[2, h], at(i, z, twin))
    for h in range(2):
        side = q // 2 if h == 0 else 1 - q // 2
        remote(prod.at[twin, side], prod.at[twin, side], pgs.at[1, h], pgr.at[1, h], at(i, z, twin)).wait_recv()
        remote(
            prod.at[far_twin, 1 - side], prod.at[far_twin, 1 - side], pgs.at[2, h], pgr.at[2, h], at(i, z, twin)
        ).wait_recv()

    def share(k, h):
        total = jnp.zeros((LANES, HALF), F32)
        for p in range(Q):
            total += jnp.dot(
                restrict[k, :, p * FINE : (p + 1) * FINE], prod[p, h], preferred_element_type=F32
            )
        return total

    half_way = nr // 2
    home = row_of(i)

    def leg(way, t, h):
        to = hop(z, 1 if way == 0 else nr - 1)
        row = home if t == half_way - 1 else i
        return remote(outgoing.at[way, t, h], incoming.at[way, t, h], fs.at[way, t, h], fr.at[way, t, h], at(row, to, q))

    for t in range(half_way):
        for other in (True, False):
            for way in range(2):
                h = 1 - way if other else way
                if t == 0 and other:
                    continue
                far_z = hop(z, half_way - t if way == 0 else nr - half_way + t)
                total = share(far_z, h)
                if t > 1 or (t == 1 and not other):
                    leg(way, t - 1, h).wait_recv()
                    total += incoming[way, t - 1, h].astype(F32)
                outgoing[way, t, h] = total.astype(BF16)
                copy = leg(way, t, h)
                copy.start()
                sent.append(copy)
        if t == 0:
            for h in range(2):
                own[h] = share(z, h)

            @pl.when(upper)
            def _():
                own_out[...] = own[...].astype(BF16)
                remote(own_out, own_in, os, orc, at(mate, z, q)).start()

    @pl.when(upper)
    def _():
        remote(own_out, own_in, os, orc, at(mate, z, q)).wait()
        own[...] = own_in[...].astype(F32)

    for h in range(2):
        total = own[h]
        for way in range(2):
            if half_way == 1 and h != way:
                continue
            leg(way, half_way - 1, h).wait_recv()
            total += incoming[way, half_way - 1, h].astype(F32)
        out_ref[:, h * HALF : (h + 1) * HALF] = total

    for copy in sent:
        copy.wait_send()
    for d in away:
        p_copy(d).wait_send()

    @pl.when(jnp.logical_not(here))
    def _():
        p_copy(0).wait_send()

    for k in range(nr):
        from_twin(far, 2, k).wait_send()

        @pl.when(k != z)
        def _():
            remote(cbuf.at[k], tbuf.at[z], c2s.at[k], c2r.at[z], at(i, k, q)).wait_send()


def solution(mesh):
    nr = mesh.shape["row"]
    ny = nr // 2

    def shards(a_values, a_rows, a_cols, a_count, p_values, p_rows, p_cols, p_count):
        dma = lambda *n: pltpu.SemaphoreType.DMA(n)
        vmem = pl.BlockSpec(memory_space=pltpu.VMEM)
        return pl.pallas_call(
            functools.partial(kernel, nr),
            out_shape=jax.ShapeDtypeStruct((CB_DEV * BS, 2 * HALF), F32),
            in_specs=[pl.BlockSpec(memory_space=pltpu.HBM)] * 8,
            out_specs=vmem,
            scratch_shapes=[
                pltpu.SMEM((1, SLOTS_A), jnp.int32),
                pltpu.SMEM((1, SLOTS_A), jnp.int32),
                pltpu.SMEM((1, 1), jnp.int32),
                pltpu.SMEM((1, SLOTS_P), jnp.int32),
                pltpu.SMEM((1, SLOTS_P), jnp.int32),
                pltpu.SMEM((1, 1), jnp.int32),
                pltpu.VMEM((1, SLOTS_A, BS * BS), BF16),
                pltpu.VMEM((1, SLOTS_P, BS * BS), BF16),
                pltpu.VMEM((SLOTS_A * BS // 2, LANES), F32),
                pltpu.VMEM((SLOTS_A * BS // 2, LANES), F32),
                pltpu.VMEM((nr, A_ROWS, LANES), BF16),
                pltpu.VMEM((nr, P_ROWS, LANES), BF16),
                pltpu.VMEM((nr, P_ROWS, LANES), BF16),
                pltpu.VMEM((Q, nr, P_ROWS, LANES), BF16),
                pltpu.VMEM((nr, FINE, SLOTS_A * BS), BF16),
                pltpu.VMEM((SLOTS_A * BS, HALF), BF16),
                pltpu.VMEM((SLOTS_A * BS, HALF), BF16),
                pltpu.VMEM((nr, LANES, Q * FINE), BF16),
                pltpu.VMEM((FINE, HALF), F32),
                pltpu.VMEM((Q, 2, FINE, HALF), BF16),
                pltpu.VMEM((2, ny, 2, LANES, HALF), BF16),
                pltpu.VMEM((2, ny, 2, LANES, HALF), BF16),
                pltpu.VMEM((2, LANES, HALF), BF16),
                pltpu.VMEM((2, LANES, HALF), BF16),
                pltpu.VMEM((2, LANES, HALF), F32),
                dma(8), dma(nr), dma(nr), dma(nr), dma(nr),
                dma(2), dma(2), dma(ny), dma(ny), dma(ny), dma(ny),
                dma(nr), dma(nr),
                dma(3, nr), dma(3, nr),
                dma(3, 2), dma(3, 2),
                dma(2, ny, 2), dma(2, ny, 2),
                pltpu.SemaphoreType.DMA, pltpu.SemaphoreType.DMA,
            ],
            compiler_params=pltpu.CompilerParams(
                collective_id=0, has_side_effects=True, vmem_limit_bytes=40 * 2**20
            ),
        )(
            a_rows, a_cols, a_count, p_rows, p_cols, p_count,
            a_values, p_values,
        )

    return jax.shard_map(
        shards,
        mesh=mesh,
        in_specs=(
            P("col", "row", None),
            P("col", "row"),
            P("col", "row"),
            P("col", "row"),
            P("row", "col", None),
            P("row", "col"),
            P("row", "col"),
            P("row", "col"),
        ),
        out_specs=P("col", "row"),
        check_vma=False,
    )
```

time: 73.6 us -> 62.9 us (0.85)
  Pallas kernels: 69.6 us -> 58.9 us
    pallas_call x1, Pallas kernels: 69.6 us -> 58.9 us  [shards(): pl.pallas_call(functools.partial(kernel, nr), out_shape=jax.ShapeDtypeStr...]
where the time goes in v3:
time: 62.9 us; the launch traced here: 62.7 us
  Pallas kernels  58.9 us (94%)
  local copies, waits for them, and re-layouts  2.38 us (4%)
  between operations  1.41 us (2%)
    pallas_call x1, Pallas kernels, shards(): pl.pallas_call(functools.partial(kernel, nr), out_shape=jax.ShapeDtypeStr...  58.9 us
    unnamed x13, local copies, waits for them, and re-layouts  2.38 us

profile of v3, /device:TPU:4, one launch (start us, length us, event | category | flops | bytes accessed | tf_op | source)
XLA Modules:
  0.0 62.7 jit_solution(7591802113559238255)
XLA Ops:
  0.0 0.0 copy-start.5
  0.7 0.0 copy-start.2
  0.7 0.0 copy-start.3
  0.7 0.0 copy-start.4
  1.4 0.0 copy-done.5
  1.4 0.0 copy-done.2
  1.4 0.0 copy-done.3
  1.4 0.0 copy-done.4
  1.4 0.0 copy-start
  1.4 0.9 %copy-done = bf16[1,16,4096]{2,1,0:T(8,128)(2,1)S(1)} copy-done((bf16[1,16,4096]{2,1,0:T(8,128)(2,1)S(1)}, bf16[1,16,4096]{2,1,0:T(8,128)(2,1)}, u32[]{:S(2)}) %copy-start) | copy-done | bytes 131096
  2.3 0.0 copy-start.1
  2.3 0.8 %copy-done.1 = bf16[1,4,4096]{2,1,0:T(4,128)(2,1)S(1)} copy-done((bf16[1,4,4096]{2,1,0:T(4,128)(2,1)S(1)}, bf16[1,4,4096]{2,1,0:T(4,128)(2,1)}, u32[]{:S(2)}) %copy-start.1) | copy-done | bytes 32792
  3.1 58.9 %shard_map.82 = f32[128,512]{1,0:T(8,128)S(1)} custom-call(s32[1,16]{1,0:T(1,128)S(1)} %copy-done.2, s32[1,16]{1,0:T(1,128)S(1)} %copy-done.3, s32[1,1]{1,0:T(1,128)S(6)} %copy.10.an_h, s32[1,4]{1,0:T(1,128)S(1)} %copy-done.4, s32[1,4]{1,0:T(1,128)S(1)} %copy-done.5, s32[1,1]{1,0:T(1,128)S(6)} %copy.11.pn_h, bf16[1,16,4096]{2,1,0:T(8,128)(2,1)S(1)} %copy-done, ...), custom_call_target="tpu_custom_call" | custom-call | tf_op jit(solution)/shard_map/pallas_call | solution.py:380
  62.0 0.7 %copy.12 = f32[128,512]{1,0:T(8,128)} copy(f32[128,512]{1,0:T(8,128)S(1)} %shard_map.82) | data formatting | bytes 524288
Async XLA Ops:
  0.0 1.4 %copy-start.5 = (s32[1,4]{1,0:T(1,128)S(1)}, s32[1,4]{1,0:T(1,128)}, u32[]{:S(2)}) copy-start(s32[1,4]{1,0:T(1,128)} %pc_h.1) | copy-start | bytes 52
  0.7 0.7 %copy-start.2 = (s32[1,16]{1,0:T(1,128)S(1)}, s32[1,16]{1,0:T(1,128)}, u32[]{:S(2)}) copy-start(s32[1,16]{1,0:T(1,128)} %ar_h.1) | copy-start | bytes 196
  0.7 0.7 %copy-start.3 = (s32[1,16]{1,0:T(1,128)S(1)}, s32[1,16]{1,0:T(1,128)}, u32[]{:S(2)}) copy-start(s32[1,16]{1,0:T(1,128)} %ac_h.1) | copy-start | bytes 196
  0.7 0.7 %copy-start.4 = (s32[1,4]{1,0:T(1,128)S(1)}, s32[1,4]{1,0:T(1,128)}, u32[]{:S(2)}) copy-start(s32[1,4]{1,0:T(1,128)} %pr_h.1) | copy-start | bytes 52
  1.4 0.9 %copy-start = (bf16[1,16,4096]{2,1,0:T(8,128)(2,1)S(1)}, bf16[1,16,4096]{2,1,0:T(8,128)(2,1)}, u32[]{:S(2)}) copy-start(bf16[1,16,4096]{2,1,0:T(8,128)(2,1)} %a_h.1) | copy-start | bytes 393220
  2.3 0.8 %copy-start.1 = (bf16[1,4,4096]{2,1,0:T(4,128)(2,1)S(1)}, bf16[1,4,4096]{2,1,0:T(4,128)(2,1)}, u32[]{:S(2)}) copy-start(bf16[1,4,4096]{2,1,0:T(4,128)(2,1)} %p_h.1) | copy-start | bytes 98308

commit v4 on v3

--- a/solution.py
+++ b/solution.py
@@ -43,7 +43,7 @@
 def kernel(
     nr,
     ar_h, ac_h, an_h, pr_h, pc_h, pn_h, a_h, p_h, out_ref,
-    ar, ac, an, pr, pc, pn, a_ref, p_ref, flat, woven, abuf, cbuf, tbuf, gbuf, left, rhs0, rhs1, restrict, acc, prod, outgoing, incoming, own_out, own_in, own,
+    ar, ac, an, pr, pc, pn, a_ref, p_ref, flat, woven, abuf, cbuf, tbuf, gbuf, left, rhs0, rhs1, restrict, acc, prod, outgoing, incoming, held, own_out, own_in, own,
     ins, zs, zr, cs, cr, asnd, arcv, ans, anr, afs, afr, c2s, c2r, b3s, b3r, pgs, pgr, fs, fr, os, orc,
 ):
     ny = nr // 2
@@ -173,10 +173,6 @@
     for e in range(1, ny):
         if e != opposite:
             launch(a_next(e, mate))
-    if opposite:
-        a_line(opposite, line(opposite)).wait_recv()
-        launch(a_mate(1, line(opposite)))
-
     for d in range(nr):
         k = hop(i, nr - d)
 
@@ -208,6 +204,23 @@
             found = sources(gbuf[first + w, k])
             for s in range(SLOTS_A):
                 rhs[pl.ds(s * BS, BS), pl.ds(w * LANES, LANES)] = pick(found, spread(cols[s : s + 1]))
+
+    if opposite:
+        a_line(opposite, line(opposite)).wait_recv()
+        launch(a_mate(1, line(opposite)))
+
+    for d in range(nr):
+        k = hop(i, nr - d)
+        if d:
+            remote(cbuf.at[k], cbuf.at[k], cs.at[k], cr.at[k], at(k, z, q)).wait_recv()
+
+        @pl.when(k == z)
+        def _():
+            tbuf[z] = cbuf[z]
+
+        @pl.when(k != z)
+        def _():
+            remote(cbuf.at[k], tbuf.at[z], c2s.at[k], c2r.at[z], at(i, k, q)).start()
 
     from_far = lambda k: remote(gbuf.at[far, k], gbuf.at[far, k], b3s.at[0, k], b3r.at[0, k], at(mate, z, far))
     from_twin = lambda p, s, k: remote(gbuf.at[p, k], gbuf.at[p, k], b3s.at[s, k], b3r.at[s, k], at(i, z, twin))
@@ -249,19 +262,6 @@
         from_far(k).wait_recv()
         from_twin(far, 2, k).start()
 
-    for d in range(nr):
-        k = hop(i, nr - d)
-        if d:
-            remote(cbuf.at[k], cbuf.at[k], cs.at[k], cr.at[k], at(k, z, q)).wait_recv()
-
-        @pl.when(k == z)
-        def _():
-            tbuf[z] = cbuf[z]
-
-        @pl.when(k != z)
-        def _():
-            remote(cbuf.at[k], tbuf.at[z], c2s.at[k], c2r.at[z], at(i, k, q)).start()
-
     for e in range(1, ny):
         if e != opposite:
             a_next(e, cross(e)).wait_recv()
@@ -310,26 +310,31 @@
     half_way = nr // 2
     home = row_of(i)
 
-    def leg(way, t, h):
+    def leg(way, t, h, g):
         to = hop(z, 1 if way == 0 else nr - 1)
         row = home if t == half_way - 1 else i
-        return remote(outgoing.at[way, t, h], incoming.at[way, t, h], fs.at[way, t, h], fr.at[way, t, h], at(row, to, q))
+        part = (way, t, h, pl.ds(g * BS, BS))
+        return remote(
+            outgoing.at[part], incoming.at[part], fs.at[way, t, h, g], fr.at[way, t, h, g], at(row, to, q)
+        )
 
     for t in range(half_way):
         for other in (True, False):
+            if t == 0 and other:
+                continue
             for way in range(2):
-                h = 1 - way if other else way
-                if t == 0 and other:
-                    continue
                 far_z = hop(z, half_way - t if way == 0 else nr - half_way + t)
-                total = share(far_z, h)
-                if t > 1 or (t == 1 and not other):
-                    leg(way, t - 1, h).wait_recv()
-                    total += incoming[way, t - 1, h].astype(F32)
-                outgoing[way, t, h] = total.astype(BF16)
-                copy = leg(way, t, h)
-                copy.start()
-                sent.append(copy)
+                held[way] = share(far_z, 1 - way if other else way)
+            for g in range(2):
+                for way in range(2):
+                    h = 1 - way if other else way
+                    rows = pl.ds(g * BS, BS)
+                    total = held[way, rows]
+                    if t > 1 or (t == 1 and not other):
+                        leg(way, t - 1, h, g).wait_recv()
+                        total += incoming[way, t - 1, h, rows].astype(F32)
+                    outgoing[way, t, h, rows] = total.astype(BF16)
+                    launch(leg(way, t, h, g))
         if t == 0:
             for h in range(2):
                 own[h] = share(z, h)
@@ -344,14 +349,16 @@
         remote(own_out, own_in, os, orc, at(mate, z, q)).wait()
         own[...] = own_in[...].astype(F32)
 
-    for h in range(2):
-        total = own[h]
-        for way in range(2):
-            if half_way == 1 and h != way:
-                continue
-            leg(way, half_way - 1, h).wait_recv()
-            total += incoming[way, half_way - 1, h].astype(F32)
-        out_ref[:, h * HALF : (h + 1) * HALF] = total
+    for g in range(2):
+        rows = pl.ds(g * BS, BS)
+        for h in range(2):
+            total = own[h, rows]
+            for way in range(2):
+                if half_way == 1 and h != way:
+                    continue
+                leg(way, half_way - 1, h, g).wait_recv()
+                total += incoming[way, half_way - 1, h, rows].astype(F32)
+            out_ref[rows, h * HALF : (h + 1) * HALF] = total
 
     for copy in sent:
         copy.wait_send()
@@ -405,6 +412,7 @@
                 pltpu.VMEM((Q, 2, FINE, HALF), BF16),
                 pltpu.VMEM((2, ny, 2, LANES, HALF), BF16),
                 pltpu.VMEM((2, ny, 2, LANES, HALF), BF16),
+                pltpu.VMEM((2, LANES, HALF), F32),
                 pltpu.VMEM((2, LANES, HALF), BF16),
                 pltpu.VMEM((2, LANES, HALF), BF16),
                 pltpu.VMEM((2, LANES, HALF), F32),
@@ -413,7 +421,7 @@
                 dma(nr), dma(nr),
                 dma(3, nr), dma(3, nr),
                 dma(3, 2), dma(3, 2),
-                dma(2, ny, 2), dma(2, ny, 2),
+                dma(2, ny, 2, 2), dma(2, ny, 2, 2),
                 pltpu.SemaphoreType.DMA, pltpu.SemaphoreType.DMA,
             ],
             compiler_params=pltpu.CompilerParams(

time: 62.9 us -> 59.1 us (0.940)
  Pallas kernels: 58.9 us -> 55.1 us
    pallas_call x1, Pallas kernels: 58.9 us -> 55.1 us  [shards(): pl.pallas_call(functools.partial(kernel, nr), out_shape=jax.ShapeDtypeStr...]
where the time goes in v4:
time: 59.1 us; the launch traced here: 58.9 us
  Pallas kernels  55.1 us (93%)
  local copies, waits for them, and re-layouts  2.38 us (4%)
  between operations  1.41 us (2%)
    pallas_call x1, Pallas kernels, shards(): pl.pallas_call(functools.partial(kernel, nr), out_shape=jax.ShapeDtypeStr...  55.1 us
    unnamed x13, local copies, waits for them, and re-layouts  2.38 us

profile of v4, /device:TPU:4, one launch (start us, length us, event | category | flops | bytes accessed | tf_op | source)
XLA Modules:
  0.0 58.9 jit_solution(1653829839060704246)
XLA Ops:
  0.0 0.0 copy-start.5
  0.7 0.0 copy-start.2
  0.7 0.0 copy-start.3
  0.7 0.0 copy-start.4
  1.4 0.0 copy-done.5
  1.4 0.0 copy-done.2
  1.4 0.0 copy-done.3
  1.4 0.0 copy-done.4
  1.4 0.0 copy-start
  1.4 0.9 %copy-done = bf16[1,16,4096]{2,1,0:T(8,128)(2,1)S(1)} copy-done((bf16[1,16,4096]{2,1,0:T(8,128)(2,1)S(1)}, bf16[1,16,4096]{2,1,0:T(8,128)(2,1)}, u32[]{:S(2)}) %copy-start) | copy-done | bytes 131096
  2.3 0.0 copy-start.1
  2.3 0.8 %copy-done.1 = bf16[1,4,4096]{2,1,0:T(4,128)(2,1)S(1)} copy-done((bf16[1,4,4096]{2,1,0:T(4,128)(2,1)S(1)}, bf16[1,4,4096]{2,1,0:T(4,128)(2,1)}, u32[]{:S(2)}) %copy-start.1) | copy-done | bytes 32792
  3.1 55.1 %shard_map.82 = f32[128,512]{1,0:T(8,128)S(1)} custom-call(s32[1,16]{1,0:T(1,128)S(1)} %copy-done.2, s32[1,16]{1,0:T(1,128)S(1)} %copy-done.3, s32[1,1]{1,0:T(1,128)S(6)} %copy.10.an_h, s32[1,4]{1,0:T(1,128)S(1)} %copy-done.4, s32[1,4]{1,0:T(1,128)S(1)} %copy-done.5, s32[1,1]{1,0:T(1,128)S(6)} %copy.11.pn_h, bf16[1,16,4096]{2,1,0:T(8,128)(2,1)S(1)} %copy-done, ...), custom_call_target="tpu_custom_call" | custom-call | tf_op jit(solution)/shard_map/pallas_call | solution.py:387
  58.2 0.7 %copy.12 = f32[128,512]{1,0:T(8,128)} copy(f32[128,512]{1,0:T(8,128)S(1)} %shard_map.82) | data formatting | bytes 524288
Async XLA Ops:
  0.0 1.4 %copy-start.5 = (s32[1,4]{1,0:T(1,128)S(1)}, s32[1,4]{1,0:T(1,128)}, u32[]{:S(2)}) copy-start(s32[1,4]{1,0:T(1,128)} %pc_h.1) | copy-start | bytes 52
  0.7 0.7 %copy-start.2 = (s32[1,16]{1,0:T(1,128)S(1)}, s32[1,16]{1,0:T(1,128)}, u32[]{:S(2)}) copy-start(s32[1,16]{1,0:T(1,128)} %ar_h.1) | copy-start | bytes 196
  0.7 0.7 %copy-start.3 = (s32[1,16]{1,0:T(1,128)S(1)}, s32[1,16]{1,0:T(1,128)}, u32[]{:S(2)}) copy-start(s32[1,16]{1,0:T(1,128)} %ac_h.1) | copy-start | bytes 196
  0.7 0.7 %copy-start.4 = (s32[1,4]{1,0:T(1,128)S(1)}, s32[1,4]{1,0:T(1,128)}, u32[]{:S(2)}) copy-start(s32[1,4]{1,0:T(1,128)} %pr_h.1) | copy-start | bytes 52
  1.4 0.9 %copy-start = (bf16[1,16,4096]{2,1,0:T(8,128)(2,1)S(1)}, bf16[1,16,4096]{2,1,0:T(8,128)(2,1)}, u32[]{:S(2)}) copy-start(bf16[1,16,4096]{2,1,0:T(8,128)(2,1)} %a_h.1) | copy-start | bytes 393220
  2.3 0.8 %copy-start.1 = (bf16[1,4,4096]{2,1,0:T(4,128)(2,1)S(1)}, bf16[1,4,4096]{2,1,0:T(4,128)(2,1)}, u32[]{:S(2)}) copy-start(bf16[1,4,4096]{2,1,0:T(4,128)(2,1)} %p_h.1) | copy-start | bytes 98308

commit v5 on v4

--- a/solution.py
+++ b/solution.py
@@ -43,8 +43,8 @@
 def kernel(
     nr,
     ar_h, ac_h, an_h, pr_h, pc_h, pn_h, a_h, p_h, out_ref,
-    ar, ac, an, pr, pc, pn, a_ref, p_ref, flat, woven, abuf, cbuf, tbuf, gbuf, left, rhs0, rhs1, restrict, acc, prod, outgoing, incoming, held, own_out, own_in, own,
-    ins, zs, zr, cs, cr, asnd, arcv, ans, anr, afs, afr, c2s, c2r, b3s, b3r, pgs, pgr, fs, fr, os, orc,
+    ar, ac, an, pr, pc, pn, a_ref, p_ref, flat, woven, abuf, cbuf, tbuf, gbuf, gkey, mykey, left, rhs0, rhs1, restrict, acc, prod, outgoing, incoming, held, own_out, own_in, own,
+    ins, ks, kr, gs, gr, zs, zr, cs, cr, asnd, arcv, ans, anr, afs, afr, c2s, c2r, b3s, b3r, pgs, pgr, fs, fr, os, orc,
 ):
     ny = nr // 2
     i = lax.axis_index("row")
@@ -111,6 +111,7 @@
         p_keys = jnp.where(rows_u == u, jnp.where(second, keys[1], keys[0]), p_keys)
     tile = jnp.concatenate([pack(p_ref, SLOTS_P), p_keys.astype(F32).astype(BF16)], axis=0)
     cbuf[i] = tile
+    mykey[...] = ((p_keys[0:1] + 1) + 64 * (p_keys[1:2] + 1)).astype(F32)
     for load in loads[4:]:
         load.wait()
     a_keys = jnp.full((KEYS, LANES), -1, jnp.int32)
@@ -135,19 +136,24 @@
         copy.start()
         sent.append(copy)
 
+    values = pl.ds(0, PAIRS_P * BS)
     p_copy = lambda d: remote(
-        cbuf.at[i], gbuf.at[q, i], zs.at[d], zr.at[i], at(row_of(z), hop(z, d), q)
+        cbuf.at[i, values], gbuf.at[q, i], zs.at[d], zr.at[i], at(row_of(z), hop(z, d), q)
     )
+    k_copy = lambda d: remote(mykey, gkey.at[q, i], ks.at[d], kr.at[i], at(row_of(z), hop(z, d), q))
     away = sorted(range(1, nr), key=lambda d: -min(d, nr - d))
     for d in away:
+        k_copy(d).start()
         p_copy(d).start()
 
     @pl.when(here)
     def _():
-        gbuf[q, i] = cbuf[i]
+        gbuf[q, i] = cbuf[i, values]
+        gkey[q, i] = mykey[...]
 
     @pl.when(jnp.logical_not(here))
     def _():
+        k_copy(0).start()
         p_copy(0).start()
 
     line = lambda e: xl * ny + (y + e) % ny
@@ -178,13 +184,14 @@
 
         @pl.when(jnp.logical_not((k == i) & here))
         def _():
-            remote(cbuf.at[i], gbuf.at[q, k], zs.at[0], zr.at[k], at(k, row_of(i), q)).wait_recv()
+            remote(mykey, gkey.at[q, k], ks.at[0], kr.at[k], at(k, row_of(i), q)).wait_recv()
+            remote(cbuf.at[i, values], gbuf.at[q, k], zs.at[0], zr.at[k], at(k, row_of(i), q)).wait_recv()
 
         send(gbuf.at[q, k], gbuf.at[q, k], b3s.at[0, k], b3r.at[0, k], at(mate, z, far))
         send(gbuf.at[q, k], gbuf.at[q, k], b3s.at[1, k], b3r.at[1, k], at(i, z, twin))
 
-    def sources(tile):
-        keys = tile[PAIRS_P * BS :].astype(F32)
+    def sources(tile, keys=None):
+        keys = tile[PAIRS_P * BS :].astype(F32) if keys is None else keys
         found = []
         for u in range(PAIRS_P):
             block = tile[u * BS : (u + 1) * BS]
@@ -201,10 +208,14 @@
     def lay(first, k, rhs):
         cols = abuf[k, pl.ds(PAIRS_A * BS + KEYS, SLOTS_A)].astype(F32)
         for w in range(2):
-            found = sources(gbuf[first + w, k])
+            code = gkey[first + w, k]
+            upper_key = jnp.floor(code * (1 / 64))
+            found = sources(gbuf[first + w, k], jnp.concatenate([code - 64 * upper_key, upper_key], axis=0) - 1)
             for s in range(SLOTS_A):
                 rhs[pl.ds(s * BS, BS), pl.ds(w * LANES, LANES)] = pick(found, spread(cols[s : s + 1]))
 
+    launch(remote(gkey.at[q], gkey.at[q], gs.at[0], gr.at[0], at(mate, z, far)))
+    launch(remote(gkey.at[q], gkey.at[q], gs.at[1], gr.at[1], at(i, z, twin)))
     if opposite:
         a_line(opposite, line(opposite)).wait_recv()
         launch(a_mate(1, line(opposite)))
@@ -256,7 +267,10 @@
             a_line(e, line(e)).wait_recv()
     for k in ours:
         place(k)
+    remote(gkey.at[twin], gkey.at[twin], gs.at[1], gr.at[1], at(i, z, twin)).wait_recv()
     multiply(side, ours, near, True)
+    remote(gkey.at[far], gkey.at[far], gs.at[0], gr.at[0], at(mate, z, far)).wait_recv()
+    launch(remote(gkey.at[far], gkey.at[far], gs.at[2], gr.at[2], at(i, z, twin)))
     for d in range(nr):
         k = hop(i, nr - d)
         from_far(k).wait_recv()
@@ -271,6 +285,7 @@
         place(k)
     multiply(side, theirs, near, False)
     share_out(side, 0)
+    remote(gkey.at[far_twin], gkey.at[far_twin], gs.at[2], gr.at[2], at(i, z, twin)).wait_recv()
     multiply(1 - side, ours + theirs, lambda k: from_twin(far_twin, 2, k).wait_recv(), True)
     share_out(1 - side, 1)
 
@@ -363,10 +378,12 @@
     for copy in sent:
         copy.wait_send()
     for d in away:
+        k_copy(d).wait_send()
         p_copy(d).wait_send()
 
     @pl.when(jnp.logical_not(here))
     def _():
+        k_copy(0).wait_send()
         p_copy(0).wait_send()
 
     for k in range(nr):
@@ -403,7 +420,9 @@
                 pltpu.VMEM((nr, A_ROWS, LANES), BF16),
                 pltpu.VMEM((nr, P_ROWS, LANES), BF16),
                 pltpu.VMEM((nr, P_ROWS, LANES), BF16),
-                pltpu.VMEM((Q, nr, P_ROWS, LANES), BF16),
+                pltpu.VMEM((Q, nr, PAIRS_P * BS, LANES), BF16),
+                pltpu.VMEM((Q, nr, 1, LANES), F32),
+                pltpu.VMEM((1, LANES), F32),
                 pltpu.VMEM((nr, FINE, SLOTS_A * BS), BF16),
                 pltpu.VMEM((SLOTS_A * BS, HALF), BF16),
                 pltpu.VMEM((SLOTS_A * BS, HALF), BF16),
@@ -416,7 +435,7 @@
                 pltpu.VMEM((2, LANES, HALF), BF16),
                 pltpu.VMEM((2, LANES, HALF), BF16),
                 pltpu.VMEM((2, LANES, HALF), F32),
-                dma(8), dma(nr), dma(nr), dma(nr), dma(nr),
+                dma(8), dma(nr), dma(nr), dma(3), dma(3), dma(nr), dma(nr), dma(nr), dma(nr),
                 dma(2), dma(2), dma(ny), dma(ny), dma(ny), dma(ny),
                 dma(nr), dma(nr),
                 dma(3, nr), dma(3, nr),

time: 59.1 us -> 58.9 us (level)
  no operation moved by 1% of the time
where the time goes in v5:
time: 58.9 us; the launch traced here: 58.8 us
  Pallas kernels  55 us (93%)
  local copies, waits for them, and re-layouts  2.38 us (4%)
  between operations  1.41 us (2%)
    pallas_call x1, Pallas kernels, shards(): pl.pallas_call(functools.partial(kernel, nr), out_shape=jax.ShapeDtypeStr...  55 us
    unnamed x13, local copies, waits for them, and re-layouts  2.38 us

profile of v5, /device:TPU:4, one launch (start us, length us, event | category | flops | bytes accessed | tf_op | source)
XLA Modules:
  0.0 58.8 jit_solution(17223681687555165345)
XLA Ops:
  0.0 0.0 copy-start.5
  0.7 0.0 copy-start.2
  0.7 0.0 copy-start.3
  0.7 0.0 copy-start.4
  1.4 0.0 copy-done.5
  1.4 0.0 copy-done.2
  1.4 0.0 copy-done.3
  1.4 0.0 copy-done.4
  1.4 0.0 copy-start
  1.4 0.9 %copy-done = bf16[1,16,4096]{2,1,0:T(8,128)(2,1)S(1)} copy-done((bf16[1,16,4096]{2,1,0:T(8,128)(2,1)S(1)}, bf16[1,16,4096]{2,1,0:T(8,128)(2,1)}, u32[]{:S(2)}) %copy-start) | copy-done | bytes 131096
  2.3 0.0 copy-start.1
  2.3 0.8 %copy-done.1 = bf16[1,4,4096]{2,1,0:T(4,128)(2,1)S(1)} copy-done((bf16[1,4,4096]{2,1,0:T(4,128)(2,1)S(1)}, bf16[1,4,4096]{2,1,0:T(4,128)(2,1)}, u32[]{:S(2)}) %copy-start.1) | copy-done | bytes 32792
  3.1 55.0 %shard_map.82 = f32[128,512]{1,0:T(8,128)S(1)} custom-call(s32[1,16]{1,0:T(1,128)S(1)} %copy-done.2, s32[1,16]{1,0:T(1,128)S(1)} %copy-done.3, s32[1,1]{1,0:T(1,128)S(6)} %copy.10.an_h, s32[1,4]{1,0:T(1,128)S(1)} %copy-done.4, s32[1,4]{1,0:T(1,128)S(1)} %copy-done.5, s32[1,1]{1,0:T(1,128)S(6)} %copy.11.pn_h, bf16[1,16,4096]{2,1,0:T(8,128)(2,1)S(1)} %copy-done, ...), custom_call_target="tpu_custom_call" | custom-call | tf_op jit(solution)/shard_map/pallas_call | solution.py:404
  58.1 0.7 %copy.12 = f32[128,512]{1,0:T(8,128)} copy(f32[128,512]{1,0:T(8,128)S(1)} %shard_map.82) | data formatting | bytes 524288
Async XLA Ops:
  0.0 1.4 %copy-start.5 = (s32[1,4]{1,0:T(1,128)S(1)}, s32[1,4]{1,0:T(1,128)}, u32[]{:S(2)}) copy-start(s32[1,4]{1,0:T(1,128)} %pc_h.1) | copy-start | bytes 52
  0.7 0.7 %copy-start.2 = (s32[1,16]{1,0:T(1,128)S(1)}, s32[1,16]{1,0:T(1,128)}, u32[]{:S(2)}) copy-start(s32[1,16]{1,0:T(1,128)} %ar_h.1) | copy-start | bytes 196
  0.7 0.7 %copy-start.3 = (s32[1,16]{1,0:T(1,128)S(1)}, s32[1,16]{1,0:T(1,128)}, u32[]{:S(2)}) copy-start(s32[1,16]{1,0:T(1,128)} %ac_h.1) | copy-start | bytes 196
  0.7 0.7 %copy-start.4 = (s32[1,4]{1,0:T(1,128)S(1)}, s32[1,4]{1,0:T(1,128)}, u32[]{:S(2)}) copy-start(s32[1,4]{1,0:T(1,128)} %pr_h.1) | copy-start | bytes 52
  1.4 0.9 %copy-start = (bf16[1,16,4096]{2,1,0:T(8,128)(2,1)S(1)}, bf16[1,16,4096]{2,1,0:T(8,128)(2,1)}, u32[]{:S(2)}) copy-start(bf16[1,16,4096]{2,1,0:T(8,128)(2,1)} %a_h.1) | copy-start | bytes 393220
  2.3 0.8 %copy-start.1 = (bf16[1,4,4096]{2,1,0:T(4,128)(2,1)S(1)}, bf16[1,4,4096]{2,1,0:T(4,128)(2,1)}, u32[]{:S(2)}) copy-start(bf16[1,4,4096]{2,1,0:T(4,128)(2,1)} %p_h.1) | copy-start | bytes 98308
